TPU v7x, 32 devices: a whole 2x2x4 slice. The times are simulated.
32 devices in a mesh: ctx: 8 (over y, x, core), exp: 4 (over z).
Axes of the slice: x: 2, y: 2, z: 4, core: 2. Of those that a mesh axis runs over, the one named last changes fastest.
Arguments:
- queries: bfloat16 [4096, 8192], P('ctx', 'exp'), may hold values from -6 to 6
- keys: bfloat16 [4096, 8192], P('ctx', 'exp'), may hold values from -6 to 6
- values: bfloat16 [4096, 8192], P('ctx', 'exp'), may hold values from -6 to 6
- log_decay: float32 [4096, 64], P('ctx', 'exp'), may hold values from -2 to 0, as said below
- residual: bfloat16 [4096, 3072], P(('ctx', 'exp')), may hold values from -6 to 6
- out_proj: bfloat16 [8192, 3072], P('exp'), may hold values from -0.0625 to 0.0625
- expert_ids: int32 [4096, 2], P(('ctx', 'exp')), may hold values from 0 to 15, all different within a row; in each aligned block of 128 rows (0 to 127, 128 to 255, ...) at most 20 rows name the same one
- route_weights: float32 [4096, 2], P(('ctx', 'exp')), may hold values from 0.1 to 0.9
- w_gate: bfloat16 [16, 3072, 6144], P('exp', None, 'ctx'), may hold values from -0.109375 to 0.109375
- w_up: bfloat16 [16, 3072, 6144], P('exp', None, 'ctx'), may hold values from -0.109375 to 0.109375
- w_down: bfloat16 [16, 6144, 3072], P('exp', 'ctx'), may hold values from -0.078125 to 0.078125
Outputs:
- mixed: bfloat16 [4096, 3072], P(('ctx', 'exp'))
Inputs may be any that keep to these rules, and one draw needn't show every extreme that they name: `expert_ids`: each token names two different experts. In each aligned block of 128 tokens no expert is named more than 20 times, and in some blocks one expert is named exactly 20 times. `log_decay`: every entry is negative.
All inputs are finite; a program needn't handle non-finite values.
Results may differ from a plain program's by a relative error of at most 0.019.
Values may be sent and summed in bfloat16 or wider, within the bound.
A program may use at most 192 MiB of HBM per device.

v0:
```python
import jax
import jax.numpy as jnp
from jax import lax
from jax.sharding import PartitionSpec as P

EPS = 1e-06


def prefix(shard, axis, combine, identity):
    length, here = (lax.axis_size(axis), lax.axis_index(axis))
    everything = jax.tree.map(
        lambda part, kind: lax.all_gather(part.astype(kind), axis),
        shard,
        (jnp.bfloat16, jnp.bfloat16),
    )
    start = jax.tree.map(
        lambda part, zero: jnp.broadcast_to(jnp.asarray(zero, part.dtype), part.shape),
        shard,
        identity,
    )

    def hop(k, before):
        reached = k < here
        new = combine(
            before, jax.tree.map(lambda part, own: part[k].astype(own.dtype), everything, shard)
        )
        return jax.tree.map(lambda a, b: jnp.where(reached, a, b), new, before)

    return lax.fori_loop(0, length, hop, start)


def chain_combine(earlier, later):
    return (earlier[0] + later[0], jnp.exp(later[0])[:, None, None] * earlier[1] + later[1])


def slot_table(chosen_specialist_index, capacity, local_experts, experts):
    flat = chosen_specialist_index.reshape(-1)
    onehot = (flat[:, None] == jnp.arange(experts, dtype=jnp.int32)[None, :]).astype(jnp.int32)
    preceding_sum = jnp.cumsum(onehot, axis=0) - onehot
    position = jnp.sum(preceding_sum * onehot, axis=1)
    slots = (
        flat // local_experts * (capacity * local_experts)
        + position * local_experts
        + flat % local_experts
    )
    return slots.reshape(chosen_specialist_index.shape)


def dispatch_table(slots, total_slots):
    assignment_tally = slots[None, :, :] == jnp.arange(total_slots, dtype=jnp.int32)[:, None, None]
    return jnp.any(assignment_tally, axis=2).astype(jnp.bfloat16)


def on_device(
    queries,
    keys,
    values,
    log_decay,
    residual,
    out_proj,
    expert_ids,
    route_weights,
    w_gate,
    w_up,
    w_down,
):
    tok = queries.shape[0]
    heads_here = log_decay.shape[1]
    head_dim = queries.shape[1] // heads_here
    q_heads = queries.reshape(tok, heads_here, head_dim)
    k_heads = keys.reshape(tok, heads_here, head_dim)
    v_heads = values.reshape(tok, heads_here, head_dim)
    cum = jnp.cumsum(log_decay, axis=0)
    scores = jnp.einsum("thd,shd->hts", q_heads, k_heads, preferred_element_type=jnp.float32)
    place = jnp.arange(tok, dtype=jnp.int32)
    causal = (place[:, None] >= place[None, :])[None]
    diff = cum.T[:, :, None] - cum.T[:, None, :]
    weights = jnp.where(causal, scores * jnp.exp(jnp.where(causal, diff, 0.0)), 0.0).astype(
        jnp.bfloat16
    )
    intra = jnp.einsum("hts,shd->thd", weights, v_heads, preferred_element_type=jnp.float32)
    last = cum[-1]
    scaled_keys = (k_heads.astype(jnp.float32) * jnp.exp(last[None, :] - cum)[:, :, None]).astype(
        jnp.bfloat16
    )
    summary = jnp.einsum("thd,the->hde", scaled_keys, v_heads, preferred_element_type=jnp.float32)
    _, carried = prefix(
        (last, summary), "ctx", chain_combine, (jnp.zeros_like(last), jnp.zeros_like(summary))
    )
    inter = jnp.exp(cum)[:, :, None] * jnp.einsum(
        "thd,hde->the", q_heads.astype(jnp.float32), carried, precision=lax.Precision.HIGHEST
    )
    attn = intra + inter
    normed = (
        (attn * lax.rsqrt(jnp.mean(attn * attn, axis=-1, keepdims=True) + EPS))
        .astype(jnp.bfloat16)
        .reshape(tok, heads_here * head_dim)
    )
    n_exp = lax.axis_size("exp")
    proj = lax.psum_scatter(
        jnp.dot(normed, out_proj, preferred_element_type=jnp.float32).astype(jnp.bfloat16),
        "exp",
        scatter_dimension=0,
        tiled=True,
    ).astype(jnp.float32)
    feature_vector = residual.astype(jnp.float32) + proj
    moe_in = (
        feature_vector
        * lax.rsqrt(jnp.mean(feature_vector * feature_vector, axis=-1, keepdims=True) + EPS)
    ).astype(jnp.bfloat16)
    local_experts = w_gate.shape[0]
    experts = local_experts * n_exp
    mtok = residual.shape[0]
    width = residual.shape[1]
    capacity = max(2, (5 * mtok + 2 * experts - 1) // (2 * experts))
    total_slots = experts * capacity
    local_slot_table = slot_table(expert_ids, capacity, local_experts, experts)
    packed = jnp.dot(
        dispatch_table(local_slot_table, total_slots), moe_in, preferred_element_type=jnp.float32
    ).astype(jnp.bfloat16)
    packed = packed.reshape(n_exp, capacity, local_experts, width)
    arrived = lax.all_to_all(packed, "exp", split_axis=0, concat_axis=1, tiled=True).reshape(
        n_exp * capacity, local_experts, width
    )
    piece = lax.all_gather(arrived, "ctx", axis=0, tiled=True)
    gate = jnp.einsum("red,edf->ref", piece, w_gate, preferred_element_type=jnp.float32)
    upper = jnp.einsum("red,edf->ref", piece, w_up, preferred_element_type=jnp.float32)
    acts = (jax.nn.silu(gate) * upper).astype(jnp.bfloat16)
    summed = lax.psum_scatter(
        jnp.einsum("ref,efd->red", acts, w_down, preferred_element_type=jnp.float32).astype(
            jnp.bfloat16
        ),
        "ctx",
        scatter_dimension=0,
        tiled=True,
    )
    outgoing = summed.reshape(n_exp, capacity, local_experts, width)
    returned = lax.all_to_all(outgoing, "exp", split_axis=0, concat_axis=0, tiled=True).reshape(
        total_slots, width
    )
    picker = (
        local_slot_table.reshape(-1)[:, None] == jnp.arange(total_slots, dtype=jnp.int32)[None, :]
    ).astype(jnp.bfloat16)
    fetched = jnp.dot(picker, returned, preferred_element_type=jnp.float32).reshape(mtok, 2, width)
    moe = route_weights[:, 0:1] * fetched[:, 0] + route_weights[:, 1:2] * fetched[:, 1]
    return (feature_vector + moe).astype(jnp.bfloat16)


def solution(mesh):
    placed = (
        P("ctx", "exp"),
        P("ctx", "exp"),
        P("ctx", "exp"),
        P("ctx", "exp"),
        P(("ctx", "exp"), None),
        P("exp", None),
        P(("ctx", "exp"), None),
        P(("ctx", "exp"), None),
        P("exp", None, "ctx"),
        P("exp", None, "ctx"),
        P("exp", "ctx", None),
    )
    return jax.shard_map(
        on_device, mesh=mesh, in_specs=placed, out_specs=P(("ctx", "exp"), None), check_vma=False
    )
```

profile of v0, /device:TPU:0, one launch (start us, length us, event | category | flops | bytes accessed | tf_op | source)
XLA Modules:
  0.0 529.2 jit_solution(10122198045515658691)
XLA Ops:
  9.2 3.9 copy.129
  13.1 3.8 fusion.25
  17.2 10.2 %all-gather.1 = bf16[8,1,16]{2,1,0:T(2,128)(2,1)S(1)} all-gather(bf16[1,1,16]{2,1,0:T(2,128)(2,1)S(1)} %bitcast.157), channel_id=1, replica_groups=mesh['ctx'=8,'exp'=4] {'ctx'}, dimensions={0}, use_global_device_ids=true | all-gather | bytes 288 | tf_op jit(solution)/shard_map/all_gather | solution.py:12
  27.5 10.3 %fusion.7 = f32[16,512,128]{1,2,0:T(8,128)} fusion(bf16[512,16,128]{0,2,1:T(8,128)(2,1)} %bitcast.154, f32[16,512]{1,0:T(8,128)S(1)} %get-tuple-element.131, pred[512,512]{1,0:T(8,128)(4,1)S(1)} %iota_compare_fusion, bf16[512,2048]{1,0:T(8,128)(2,1)} %param.15, bf16[512,2048]{1,0:T(8,128)(2,1)S(1)} %copy-done), kind=kOutput, calls=%fused_computation.20 | convolution fusion | flops 2168455168 | bytes 10780672 | tf_op jit(solution)/shard_map/hts,shd->thd/dot_general | solution.py:81
  37.8 18.7 %all-gather.7.cloned.1.call-done = bf16[128,128,128]{2,1,0:T(8,128)(2,1)} async-done(((bf16[16,128,128]{2,1,0:T(8,128)(2,1)}), bf16[128,128,128]{2,1,0:T(8,128)(2,1)}) %all-gather.7.cloned.1.call-update) | async-done | bytes 4194320 | tf_op jit(solution)/shard_map/all_gather | solution.py:12
  56.5 10.6 %while.14 = (s32[]{:T(128)}, f32[16,128,128]{2,1,0:T(8,128)S(1)}, s32[]{:T(128)}, bf16[8,16]{1,0:T(8,128)(2,1)S(1)}, bf16[8,16,128,128]{3,2,1,0:T(8,128)(2,1)}, /*index=5*/s32[]{:T(128)}, s32[]{:T(128)}) while((s32[]{:T(128)}, f32[16,128,128]{2,1,0:T(8,128)S(1)}, s32[]{:T(128)}, bf16[8,16]{1,0:T(8,128)(2,1)S(1)}, ...), condition=%wide.region_3.4_spmd.clone, body=%wide.region_2.3_spmd.clone.sunk | while | flops 1310740 | bytes 2621705 | solution.py:29
  56.5 1.3 fusion.61
  57.9 1.3 fusion.61
  59.2 1.3 fusion.61
  60.5 1.3 fusion.61
  61.8 1.3 fusion.61
  63.2 1.3 fusion.61
  64.5 1.3 fusion.61
  67.1 4.5 multiply_reduce_fusion
  72.3 11.0 %convolution_convert_fusion = bf16[512,3072]{1,0:T(8,128)(2,1)} fusion(bf16[512,2048]{0,1:T(8,128)(2,1)S(1)} %bitcast.152, bf16[2048,3072]{1,0:T(8,128)(2,1)} %param.18), kind=kOutput, calls=%fused_computation.12 | convolution fusion | flops 6444023808 | bytes 17825792 | tf_op jit(solution)/shard_map/dot_general | solution.py:101
  85.6 58.1 %reduce-scatter.3.cloned.1.call-done = bf16[128,3072]{1,0:T(8,128)(2,1)} async-done(((bf16[512,3072]{1,0:T(8,128)(2,1)}), bf16[128,3072]{1,0:T(8,128)(2,1)}) %reduce-scatter.3.cloned.1.call-update) | async-done | bytes 786448 | tf_op jit(solution)/shard_map/reduce_scatter | solution.py:100
  143.7 1.5 multiply_reduce_fusion.1
  145.2 3.2 convolution_convert_fusion.1
  148.4 3.2 reshape.234
  151.6 49.0 %all_to_all.14 = bf16[4,20,4,3072]{3,2,1,0:T(4,128)(2,1)S(1)} all-to-all(bf16[4,20,4,3072]{3,2,1,0:T(4,128)(2,1)S(1)} %reshape.234), channel_id=1, replica_groups=mesh['ctx'=8,'exp'=4] {'exp'}, dimensions={0} | all-to-all | bytes 3932160 | tf_op jit(solution)/shard_map/all_to_all | solution.py:122
  200.6 1.9 copy.125
  202.5 84.7 %all-gather.5.cloned.1.call-done = bf16[640,4,3072]{2,0,1:T(8,128)(2,1)} async-done(((bf16[80,4,3072]{2,0,1:T(8,128)(2,1)}), bf16[640,4,3072]{2,0,1:T(8,128)(2,1)}) %all-gather.5.cloned.1.call-update) | async-done | bytes 15728656 | tf_op jit(solution)/shard_map/all_gather | solution.py:125
  287.2 21.5 %fusion.42 = f32[4,640,768]{2,1,0:T(8,128)} fusion(bf16[640,4,3072]{2,0,1:T(8,128)(2,1)} %all-gather.5.cloned.1.call-done, bf16[4,3072,768]{2,1,0:T(8,128)(2,1)} %param.22), kind=kOutput, calls=%fused_computation.81 | convolution fusion | flops 12079595520 | bytes 42467328 | tf_op jit(solution)/shard_map/red,edf->ref/dot_general | solution.py:127
  308.7 23.9 %fusion.1 = bf16[640,4,768]{2,0,1:T(8,128)(2,1)} fusion(f32[4,640,768]{2,1,0:T(8,128)} %fusion.42, bf16[640,4,3072]{2,0,1:T(8,128)(2,1)} %all-gather.5.cloned.1.call-done, bf16[4,3072,768]{2,1,0:T(8,128)(2,1)} %param.21), kind=kOutput, calls=%fused_computation.6 | convolution fusion | flops 12091392000 | bytes 46399488 | tf_op jit(solution)/shard_map/red,edf->ref/dot_general | solution.py:126
  332.6 20.7 %convert_bitcast_fusion = bf16[640,4,3072]{2,0,1:T(8,128)(2,1)} fusion(bf16[640,4,768]{2,0,1:T(8,128)(2,1)} %fusion.1, bf16[4,768,3072]{2,1,0:T(8,128)(2,1)} %param.23), kind=kOutput, calls=%fused_computation.4 | convolution fusion | flops 12087459840 | bytes 38535168 | tf_op jit(solution)/shard_map/ref,efd->red/dot_general | solution.py:130
  353.3 109.3 %reduce-scatter.5.cloned.1.call-done = bf16[80,4,3072]{2,0,1:T(8,128)(2,1)} async-done(((bf16[640,4,3072]{2,0,1:T(8,128)(2,1)}), bf16[80,4,3072]{2,0,1:T(8,128)(2,1)}) %reduce-scatter.5.cloned.1.call-update) | async-done | bytes 1966096 | tf_op jit(solution)/shard_map/reduce_scatter | solution.py:129
  462.7 4.3 copy.126
  467.0 4.6 all-to-all-start.1
  471.6 45.4 %all-to-all-done.1 = bf16[4,20,4,3072]{3,2,1,0:T(4,128)(2,1)S(1)} async-done(((bf16[4,20,4,3072]{3,2,1,0:T(4,128)(2,1)}), bf16[4,20,4,3072]{3,2,1,0:T(4,128)(2,1)S(1)}, u32[]{:S(2)}, u32[]{:S(2)}) %all-to-all-start.1) | async-done | bytes 1966112 | tf_op jit(solution)/shard_map/all_to_all | solution.py:138
  517.0 1.5 reshape.243
  518.5 2.7 fusion.30
  521.3 1.4 fusion.23
  (59 shorter events, 7.3 us)
Async XLA Ops:
  6.5 20.9 %copy-start = (bf16[512,2048]{1,0:T(8,128)(2,1)S(1)}, bf16[512,2048]{1,0:T(8,128)(2,1)}, u32[]{:S(2)}) copy-start(bf16[512,2048]{1,0:T(8,128)(2,1)} %param.13) | copy-start | bytes 6291460
  6.5 50.0 %all-gather.7.cloned.1.call-start = ((), (), s32[]{:S(2)}) async-start(), calls=%async_computation.7 | async-start | bytes 4718592 | tf_op jit(solution)/shard_map/all_gather | solution.py:12
  16.9 126.8 %reduce-scatter.3.cloned.1.call-start = ((), (), s32[]{:S(2)}) async-start(), calls=%async_computation.4 | async-start | bytes 3932160 | tf_op jit(solution)/shard_map/reduce_scatter | solution.py:100
  83.3 0.7 copy-start.4
  83.3 60.4 %copy-start.2 = (bf16[128,3072]{1,0:T(8,128)(2,1)S(1)}, bf16[128,3072]{1,0:T(8,128)(2,1)}, u32[]{:S(2)}) copy-start(bf16[128,3072]{1,0:T(8,128)(2,1)} %param.17) | copy-start | bytes 2359300
  83.3 203.9 %all-gather.5.cloned.1.call-start = ((), (), s32[]{:S(2)}) async-start(), calls=%async_computation.5 | async-start | bytes 17694720 | tf_op jit(solution)/shard_map/all_gather | solution.py:125
  202.4 260.2 %reduce-scatter.5.cloned.1.call-start = ((), (), s32[]{:S(2)}) async-start(), calls=%async_computation.6 | async-start | bytes 17694720 | tf_op jit(solution)/shard_map/reduce_scatter | solution.py:129
  353.3 118.3 %copy-start.5 = (f32[128,2]{0,1:T(2,128)S(1)}, f32[128,2]{0,1:T(2,128)}, u32[]{:S(2)}) copy-start(f32[128,2]{0,1:T(2,128)} %param.20) | copy-start | bytes 3076
  467.0 50.0 %all-to-all-start.1 = ((bf16[4,20,4,3072]{3,2,1,0:T(4,128)(2,1)}), bf16[4,20,4,3072]{3,2,1,0:T(4,128)(2,1)S(1)}, u32[]{:S(2)}, u32[]{:S(2)}) async-start(bf16[4,20,4,3072]{3,2,1,0:T(4,128)(2,1)} %bitcast.150), calls=%async_computation.3 | async-start | bytes 3932160 | tf_op jit(solution)/shard_map/all_to_all | solution.py:138
  518.5 2.7 copy-start.3
  518.5 4.2 copy-start.1
Sparse Core Ops, SparseCore 0:
  17.1 39.4 all-gather.6
  83.5 60.2 reduce-scatter.2
  202.6 84.5 all-gather.4
  353.5 109.1 reduce-scatter.4
where the time goes:
time: 530 us; the launch traced here: 529 us
  waiting for transfers between devices  316 us (60%)
  matrix products  102 us (19%)
  blocking collectives  59.2 us (11%)
  local copies, waits for them, and re-layouts  17.5 us (3%)
  other arithmetic  16.2 us (3%)
  between operations  13.3 us (3%)
    reduce_scatter x1, waiting for transfers between devices, on_device(): lax.psum_scatter(jnp.einsum('ref,efd->red', acts, w_down, preferred_eleme...  109 us
    all_gather x1, waiting for transfers between devices, on_device(): piece = lax.all_gather(arrived, 'ctx', axis=0, tiled=True)  84.7 us
    reduce_scatter x1, waiting for transfers between devices, on_device(): lax.psum_scatter(jnp.dot(normed, out_proj, preferred_element_type=jnp.flo...  58.1 us
    all_to_all x1, blocking collectives, on_device(): lax.all_to_all(packed, 'exp', split_axis=0, concat_axis=1, tiled=True)  49 us
    all_to_all x1, waiting for transfers between devices, on_device(): lax.all_to_all(outgoing, 'exp', split_axis=0, concat_axis=0, tiled=True)  45.4 us
    dot_general x1, matrix products, on_device(): jnp.einsum('red,edf->ref', piece, w_gate, preferred_element_type=jnp.floa...  23.9 us
    dot_general x1, matrix products, on_device(): jnp.einsum('red,edf->ref', piece, w_up, preferred_element_type=jnp.float32)  21.5 us
    dot_general x1, matrix products, on_device(): jnp.einsum('ref,efd->red', acts, w_down, preferred_element_type=jnp.float32)  20.7 us
  transfers between devices with their start and end apart: 5, of which 5 were waited for; matrix products, arithmetic and copies ran while one was open for 2% of the time, Pallas kernels for 0%

commit v1 on v0

--- a/solution.py
+++ b/solution.py
@@ -1,6 +1,8 @@
 import jax
 import jax.numpy as jnp
 from jax import lax
+from jax.experimental import pallas as pl
+from jax.experimental.pallas import tpu as pltpu
 from jax.sharding import PartitionSpec as P
 
 EPS = 1e-06
@@ -33,11 +35,23 @@
     return (earlier[0] + later[0], jnp.exp(later[0])[:, None, None] * earlier[1] + later[1])
 
 
-def slot_table(chosen_specialist_index, capacity, local_experts, experts):
+def slot_table(chosen_specialist_index, capacity, local_experts, experts, tiled):
     flat = chosen_specialist_index.reshape(-1)
     onehot = (flat[:, None] == jnp.arange(experts, dtype=jnp.int32)[None, :]).astype(jnp.int32)
-    preceding_sum = jnp.cumsum(onehot, axis=0) - onehot
+    earlier = jnp.tri(flat.shape[0], k=-1, dtype=jnp.bfloat16)
+    preceding_sum = jnp.dot(
+        earlier, onehot.astype(jnp.bfloat16), preferred_element_type=jnp.float32
+    ).astype(jnp.int32)
     position = jnp.sum(preceding_sum * onehot, axis=1)
+    if tiled:
+        few = capacity - TILE
+        here = flat % local_experts
+        slots = flat // local_experts * (capacity * local_experts) + jnp.where(
+            position < TILE,
+            few * local_experts + TILE * here + position,
+            few * here + position - TILE,
+        )
+        return slots.reshape(chosen_specialist_index.shape)
     slots = (
         flat // local_experts * (capacity * local_experts)
         + position * local_experts
@@ -49,6 +63,327 @@
 def dispatch_table(slots, total_slots):
     assignment_tally = slots[None, :, :] == jnp.arange(total_slots, dtype=jnp.int32)[:, None, None]
     return jnp.any(assignment_tally, axis=2).astype(jnp.bfloat16)
+
+
+TILE = 16
+PARTS = 5
+
+
+def expert_kernel(
+    packed, w_gate, w_up, w_down, out,
+    rows, extra, acts, extra_acts, pair, diag_x, diag_y, sum_x, sum_y, final, w_in, w_out,
+    z_send, z_recv, g_send, g_recv, r_send, r_recv, b_send, b_recv, w_sem, d_sem,
+):
+    me, z = lax.axis_index("ctx"), lax.axis_index("exp")
+    core, x, y = me % 2, (me // 2) % 2, me // 4
+    mate = (me + 1 - 2 * core, z)
+    x_near = (me + 2 - 4 * x, z)
+    y_near = (me + 4 - 8 * y, z)
+    others = [(me, (z + k) % 4) for k in (1, 2, 3)]
+    block, width = rows.shape[3], rows.shape[4]
+    half = block // 2
+    experts = w_gate.shape[0]
+    hidden = w_gate.shape[2]
+    tile, wide = w_in.shape[3], w_out.shape[2]
+    tiles, wides = hidden // tile, width // wide
+    top, bottom = pl.ds(0, half), pl.ds(half, half)
+
+    barrier = pltpu.get_barrier_semaphore()
+    for device in [mate, x_near, y_near] + others:
+        pl.semaphore_signal(
+            barrier, inc=1, device_id=device, device_id_type=pl.DeviceIdType.MESH
+        )
+    pl.semaphore_wait(barrier, 6)
+
+    def remote(src, dst, send, recv, device):
+        return pltpu.make_async_remote_copy(
+            src_ref=src, dst_ref=dst, send_sem=send, recv_sem=recv,
+            device_id=device, device_id_type=pl.DeviceIdType.MESH,
+        )
+
+    def part_rows(p):
+        return pl.ds(pl.multiple_of(p * TILE, TILE), TILE)
+
+    def z_copy(p, k):
+        return remote(
+            packed.at[others[k][1], part_rows(p)], rows.at[p, 0, 0, part_rows(z)],
+            z_send.at[p, k], z_recv.at[p, k], others[k],
+        )
+
+    def g_copy(p, k):
+        src, dst, device = (
+            lambda: (rows.at[p, 0, 0], rows.at[p, 0, 1], x_near),
+            lambda: (rows.at[p, 0, 0], rows.at[p, 0, 2], y_near),
+            lambda: (rows.at[p, 0, 0], rows.at[p, 1, 0], mate),
+            lambda: (rows.at[p, 0, 1, top], rows.at[p, 0, 3, top], y_near),
+            lambda: (rows.at[p, 0, 2, bottom], rows.at[p, 0, 3, bottom], x_near),
+            lambda: (rows.at[p, 0, 1], rows.at[p, 1, 1], mate),
+            lambda: (rows.at[p, 0, 2], rows.at[p, 1, 2], mate),
+            lambda: (rows.at[p, 0, 3], rows.at[p, 1, 3], mate),
+        )[k]()
+        return remote(src, dst, g_send.at[p, k], g_recv.at[p, k], device)
+
+    def r_copy(p, k):
+        src, dst, device = (
+            lambda: (rows.at[p, 1], pair.at[p], mate),
+            lambda: (rows.at[p, 0, 3, top], diag_x.at[p], x_near),
+            lambda: (rows.at[p, 0, 3, bottom], diag_y.at[p], y_near),
+            lambda: (rows.at[p, 0, 1], sum_x.at[p], x_near),
+            lambda: (rows.at[p, 0, 2], sum_y.at[p], y_near),
+        )[k]()
+        return remote(src, dst, r_send.at[p, k], r_recv.at[p, k], device)
+
+    def b_copy(p, k):
+        return remote(
+            final.at[p, part_rows(others[k][1])], out.at[z, part_rows(p)],
+            b_send.at[p, k], b_recv.at[p, k], others[k],
+        )
+
+    def gather_1(p):
+        for k in range(3):
+            z_copy(p, k).wait_recv()
+        for k in (0, 1, 2):
+            g_copy(p, k).start()
+
+    def gather_2(p):
+        g_copy(p, 0).wait_recv()
+        g_copy(p, 3).start()
+        g_copy(p, 5).start()
+        g_copy(p, 1).wait_recv()
+        g_copy(p, 4).start()
+        g_copy(p, 6).start()
+
+    def gather_3(p):
+        g_copy(p, 3).wait_recv()
+        g_copy(p, 4).wait_recv()
+        g_copy(p, 7).start()
+
+    def gather_4(p):
+        for k in (2, 5, 6, 7):
+            g_copy(p, k).wait_recv()
+
+    def gather_sent(p):
+        for k in range(8):
+            g_copy(p, k).wait_send()
+
+    def add(a, b):
+        return a.astype(jnp.float32) + b.astype(jnp.float32)
+
+    def reduce_1(p):
+        r_copy(p, 0).start()
+
+    def reduce_2(p):
+        r_copy(p, 0).wait_recv()
+        for q in (3, 1, 2, 0):
+            rows[p, 0, q] = add(rows[p, 0, q], pair[p, q]).astype(jnp.bfloat16)
+            if q == 3:
+                r_copy(p, 1).start()
+                r_copy(p, 2).start()
+
+    def reduce_3(p):
+        r_copy(p, 1).wait_recv()
+        rows[p, 0, 2, top] = add(rows[p, 0, 2, top], diag_x[p]).astype(jnp.bfloat16)
+        r_copy(p, 4).start()
+        r_copy(p, 2).wait_recv()
+        rows[p, 0, 1, bottom] = add(rows[p, 0, 1, bottom], diag_y[p]).astype(jnp.bfloat16)
+        r_copy(p, 3).start()
+
+    def reduce_4(p):
+        r_copy(p, 3).wait_recv()
+        r_copy(p, 4).wait_recv()
+        total = add(rows[p, 0, 0], sum_x[p]) + sum_y[p].astype(jnp.float32)
+        final[p] = total.astype(jnp.bfloat16)
+        for k in range(3):
+            b_copy(p, k).start()
+        out[z, part_rows(p)] = final[p, part_rows(z)]
+
+    def in_copies(n):
+        e, cols = n // tiles, pl.ds(pl.multiple_of((n % tiles) * tile, tile), tile)
+        return [
+            pltpu.make_async_copy(w.at[e, :, cols], w_in.at[n % 2, i], w_sem.at[n % 2, i])
+            for i, w in enumerate((w_gate, w_up))
+        ]
+
+    def out_copy(n):
+        cols = pl.ds(pl.multiple_of((n % wides) * wide, wide), wide)
+        return pltpu.make_async_copy(
+            w_down.at[n // wides, :, cols], w_out.at[n % 2], d_sem.at[n % 2]
+        )
+
+    for p in range(PARTS):
+        for k in range(3):
+            z_copy(p, k).start()
+    for n in range(2):
+        for copy in in_copies(n):
+            copy.start()
+        out_copy(n).start()
+    for p in range(PARTS):
+        rows[p, 0, 0, part_rows(z)] = packed[z, part_rows(p)]
+
+    gather_1(0)
+    gather_1(1)
+    gather_2(0)
+    gather_1(2)
+    gather_2(1)
+    gather_3(0)
+    gather_4(0)
+
+    total_rows = 8 * block
+    per = total_rows // experts
+    few = TILE // experts
+    here = lax.broadcasted_iota(jnp.int32, (total_rows, total_rows), 0)
+    there = lax.broadcasted_iota(jnp.int32, (total_rows, total_rows), 1)
+
+    place = ((here % per) // few) * TILE + (here // per) * few + here % few
+    pick = (place == there).astype(jnp.bfloat16)
+
+    @pl.loop(0, wides)
+    def _(n):
+        cols = pl.ds(pl.multiple_of(n * wide, wide), wide)
+        had = rows[0, :, :, :, cols].reshape(total_rows, wide)
+        extra[:, :, cols] = (
+            jnp.dot(pick, had, preferred_element_type=jnp.float32)
+            .astype(jnp.bfloat16)
+            .reshape(experts, per, wide)
+        )
+
+    gather_3(1)
+    gather_1(3)
+
+    def silu_times(a, n):
+        gate = jnp.dot(a, w_in[n % 2, 0], preferred_element_type=jnp.float32)
+        upper = jnp.dot(a, w_in[n % 2, 1], preferred_element_type=jnp.float32)
+        return (gate / (1.0 + jnp.exp(-gate)) * upper).astype(jnp.bfloat16)
+
+    @pl.loop(0, experts)
+    def _(e):
+        p = e + 1
+        gather_4(p)
+
+        @pl.loop(0, tiles)
+        def _(s):
+            n = e * tiles + s
+            for copy in in_copies(n):
+                copy.wait()
+            acts[s] = silu_times(rows[p].reshape(total_rows, width), n)
+            extra_acts[s] = silu_times(extra[e], n)
+
+            @pl.when(n + 2 < experts * tiles)
+            def _():
+                for copy in in_copies(n + 2):
+                    copy.start()
+
+            @pl.when((s == 0) & (e < experts - 1))
+            def _():
+                gather_2(p + 1)
+
+            @pl.when((s == 0) & (e == 0))
+            def _():
+                gather_1(4)
+
+            @pl.when((s == 1) & (e < experts - 1))
+            def _():
+                gather_3(p + 1)
+
+            @pl.when((s == 0) & (e > 0))
+            def _():
+                reduce_2(p - 1)
+
+            @pl.when((s == 1) & (e > 0))
+            def _():
+                reduce_3(p - 1)
+
+            @pl.when((s == 2) & (e > 0))
+            def _():
+                reduce_4(p - 1)
+
+        gather_sent(p)
+
+        @pl.loop(0, wides)
+        def _(s):
+            n = e * wides + s
+            out_copy(n).wait()
+            cols = pl.ds(pl.multiple_of(s * wide, wide), wide)
+
+            def down(ref):
+                return sum(
+                    jnp.dot(
+                        ref[i], w_out[n % 2, i * tile:(i + 1) * tile, :],
+                        preferred_element_type=jnp.float32,
+                    )
+                    for i in range(tiles)
+                ).astype(jnp.bfloat16)
+
+            rows[p, :, :, :, cols] = down(acts).reshape(2, 4, block, wide)
+            extra[e, :, cols] = down(extra_acts)
+
+            @pl.when(n + 2 < experts * wides)
+            def _():
+                out_copy(n + 2).start()
+
+        reduce_1(p)
+
+    gather_sent(0)
+    back = ((there % per) // few) * TILE + (there // per) * few + there % few
+    unpick = (back == here).astype(jnp.bfloat16)
+
+    @pl.loop(0, wides)
+    def _(n):
+        cols = pl.ds(pl.multiple_of(n * wide, wide), wide)
+        made = extra[:, :, cols].reshape(total_rows, wide)
+        rows[0, :, :, :, cols] = (
+            jnp.dot(unpick, made, preferred_element_type=jnp.float32)
+            .astype(jnp.bfloat16)
+            .reshape(2, 4, block, wide)
+        )
+
+    reduce_1(0)
+    for stage in (reduce_2, reduce_3, reduce_4):
+        stage(4)
+        stage(0)
+    for p in range(PARTS):
+        for k in range(3):
+            z_copy(p, k).wait_send()
+            b_copy(p, k).wait()
+        for k in range(5):
+            r_copy(p, k).wait_send()
+
+
+def expert_layer(packed, w_gate, w_up, w_down):
+    experts, width, hidden = w_gate.shape
+    block = 4 * TILE
+    tile, wide = hidden // 3, width // 3
+    bf16, dma = jnp.bfloat16, pltpu.SemaphoreType.DMA
+    anywhere = pl.BlockSpec(memory_space=pl.ANY)
+    vmem = pl.BlockSpec(memory_space=pltpu.VMEM)
+    return pl.pallas_call(
+        expert_kernel,
+        out_shape=jax.ShapeDtypeStruct(packed.shape, bf16),
+        in_specs=[vmem, anywhere, anywhere, anywhere],
+        out_specs=vmem,
+        scratch_shapes=[
+            pltpu.VMEM((PARTS, 2, 4, block, width), bf16),
+            pltpu.VMEM((experts, 8 * block // experts, width), bf16),
+            pltpu.VMEM((3, 8 * block, tile), bf16),
+            pltpu.VMEM((3, 8 * block // experts, tile), bf16),
+            pltpu.VMEM((PARTS, 4, block, width), bf16),
+            pltpu.VMEM((PARTS, block // 2, width), bf16),
+            pltpu.VMEM((PARTS, block // 2, width), bf16),
+            pltpu.VMEM((PARTS, block, width), bf16),
+            pltpu.VMEM((PARTS, block, width), bf16),
+            pltpu.VMEM((PARTS, block, width), bf16),
+            pltpu.VMEM((2, 2, width, tile), bf16),
+            pltpu.VMEM((2, hidden, wide), bf16),
+            dma((PARTS, 3)), dma((PARTS, 3)),
+            dma((PARTS, 8)), dma((PARTS, 8)),
+            dma((PARTS, 5)), dma((PARTS, 5)),
+            dma((PARTS, 3)), dma((PARTS, 3)),
+            dma((2, 2)), dma((2,)),
+        ],
+        compiler_params=pltpu.CompilerParams(
+            collective_id=0, has_side_effects=True, vmem_limit_bytes=60 * 1024 * 1024
+        ),
+    )(packed, w_gate, w_up, w_down)
 
 
 def on_device(
@@ -70,7 +405,9 @@
     q_heads = queries.reshape(tok, heads_here, head_dim)
     k_heads = keys.reshape(tok, heads_here, head_dim)
     v_heads = values.reshape(tok, heads_here, head_dim)
-    cum = jnp.cumsum(log_decay, axis=0)
+    cum = jnp.dot(
+        jnp.tri(tok, dtype=jnp.float32), log_decay, precision=lax.Precision.HIGHEST
+    )
     scores = jnp.einsum("thd,shd->hts", q_heads, k_heads, preferred_element_type=jnp.float32)
     place = jnp.arange(tok, dtype=jnp.int32)
     causal = (place[:, None] >= place[None, :])[None]
@@ -114,30 +451,37 @@
     width = residual.shape[1]
     capacity = max(2, (5 * mtok + 2 * experts - 1) // (2 * experts))
     total_slots = experts * capacity
-    local_slot_table = slot_table(expert_ids, capacity, local_experts, experts)
+    n_ctx = lax.axis_size("ctx")
+    tiled = (n_ctx, n_exp, local_experts, capacity) == (8, 4, 4, TILE + 4)
+    local_slot_table = slot_table(expert_ids, capacity, local_experts, experts, tiled)
     packed = jnp.dot(
         dispatch_table(local_slot_table, total_slots), moe_in, preferred_element_type=jnp.float32
     ).astype(jnp.bfloat16)
-    packed = packed.reshape(n_exp, capacity, local_experts, width)
-    arrived = lax.all_to_all(packed, "exp", split_axis=0, concat_axis=1, tiled=True).reshape(
-        n_exp * capacity, local_experts, width
-    )
-    piece = lax.all_gather(arrived, "ctx", axis=0, tiled=True)
-    gate = jnp.einsum("red,edf->ref", piece, w_gate, preferred_element_type=jnp.float32)
-    upper = jnp.einsum("red,edf->ref", piece, w_up, preferred_element_type=jnp.float32)
-    acts = (jax.nn.silu(gate) * upper).astype(jnp.bfloat16)
-    summed = lax.psum_scatter(
-        jnp.einsum("ref,efd->red", acts, w_down, preferred_element_type=jnp.float32).astype(
-            jnp.bfloat16
-        ),
-        "ctx",
-        scatter_dimension=0,
-        tiled=True,
-    )
-    outgoing = summed.reshape(n_exp, capacity, local_experts, width)
-    returned = lax.all_to_all(outgoing, "exp", split_axis=0, concat_axis=0, tiled=True).reshape(
-        total_slots, width
-    )
+    if tiled:
+        returned = expert_layer(
+            packed.reshape(n_exp, capacity * local_experts, width), w_gate, w_up, w_down
+        ).reshape(total_slots, width)
+    else:
+        packed = packed.reshape(n_exp, capacity, local_experts, width)
+        arrived = lax.all_to_all(packed, "exp", split_axis=0, concat_axis=1, tiled=True).reshape(
+            n_exp * capacity, local_experts, width
+        )
+        piece = lax.all_gather(arrived, "ctx", axis=0, tiled=True)
+        gate = jnp.einsum("red,edf->ref", piece, w_gate, preferred_element_type=jnp.float32)
+        upper = jnp.einsum("red,edf->ref", piece, w_up, preferred_element_type=jnp.float32)
+        acts = (jax.nn.silu(gate) * upper).astype(jnp.bfloat16)
+        summed = lax.psum_scatter(
+            jnp.einsum("ref,efd->red", acts, w_down, preferred_element_type=jnp.float32).astype(
+                jnp.bfloat16
+            ),
+            "ctx",
+            scatter_dimension=0,
+            tiled=True,
+        )
+        outgoing = summed.reshape(n_exp, capacity, local_experts, width)
+        returned = lax.all_to_all(outgoing, "exp", split_axis=0, concat_axis=0, tiled=True).reshape(
+            total_slots, width
+        )
     picker = (
         local_slot_table.reshape(-1)[:, None] == jnp.arange(total_slots, dtype=jnp.int32)[None, :]
     ).astype(jnp.bfloat16)

time: 530 us -> 348 us (0.66)
  waiting for transfers between devices: 316 us -> 77.7 us
  Pallas kernels: 0 us -> 189 us
  matrix products: 102 us -> 35.9 us
  blocking collectives: 59.2 us -> 10.2 us
  local copies, waits for them, and re-layouts: 17.5 us -> 5.69 us
    pallas_call x0 -> x1, Pallas kernels: none -> 189 us  [expert_layer(): pl.pallas_call(expert_kernel, out_shape=jax.ShapeDtypeStruct(packed.shape...]
    reduce_scatter x1 -> x0, waiting for transfers between devices: 109 us -> none  [on_device(): lax.psum_scatter(jnp.einsum('ref,efd->red', acts, w_down, preferred_eleme...]
    all_gather x1 -> x0, waiting for transfers between devices: 84.7 us -> none  [on_device(): piece = lax.all_gather(arrived, 'ctx', axis=0, tiled=True)]
    dot_general x3 -> x2, matrix products: 66.1 us -> 1.57 us  [the longest x1 1.29 us: on_device(): jnp.dot(jnp.tri(tok, dtype=jnp.float32), log_decay, precision=lax.Precisi...]
    all_to_all x1 -> x0, blocking collectives: 49 us -> none  [on_device(): lax.all_to_all(packed, 'exp', split_axis=0, concat_axis=1, tiled=True)]
    all_to_all x1 -> x0, waiting for transfers between devices: 45.4 us -> none  [on_device(): lax.all_to_all(outgoing, 'exp', split_axis=0, concat_axis=0, tiled=True)]
    reshape x4 -> x0, local copies, waits for them, and re-layouts: 7.49 us -> none  [the longest x1 3.22 us: on_device(): packed = packed.reshape(n_exp, capacity, local_experts, width)]
  transfers between devices with their start and end apart: 5 -> 2, of which waited for: 5 -> 2; matrix products, arithmetic and copies ran while one was open for 2% -> 3% of each run, Pallas kernels for 0% -> 0%
where the time goes in v1:
time: 348 us; the launch traced here: 346 us
  Pallas kernels  189 us (54%)
  waiting for transfers between devices  77.7 us (22%)
  matrix products  35.9 us (10%)
  other arithmetic  14.3 us (4%)
  between operations  13.6 us (4%)
  blocking collectives  10.2 us (3%)
  local copies, waits for them, and re-layouts  5.69 us (2%)
    pallas_call x1, Pallas kernels, expert_layer(): pl.pallas_call(expert_kernel, out_shape=jax.ShapeDtypeStruct(packed.shape...  189 us
    reduce_scatter x1, waiting for transfers between devices, on_device(): lax.psum_scatter(jnp.dot(normed, out_proj, preferred_element_type=jnp.flo...  58.9 us
    all_gather x1, waiting for transfers between devices, prefix(): lax.all_gather(part.astype(kind), axis)  18.7 us
    dot_general x1, matrix products, on_device(): jnp.dot(normed, out_proj, preferred_element_type=jnp.float32)  11 us
    select_n x8, other arithmetic, hop(): return jax.tree.map(lambda a, b: jnp.where(reached, a, b), new, before)  10.3 us
    dot_general x1, matrix products, on_device(): jnp.einsum('hts,shd->thd', weights, v_heads, preferred_element_type=jnp.f...  10.3 us
    all_gather x1, blocking collectives, prefix(): lax.all_gather(part.astype(kind), axis)  10.2 us
  transfers between devices with their start and end apart: 2, of which 2 were waited for; matrix products, arithmetic and copies ran while one was open for 3% of the time, Pallas kernels for 0%

profile of v1, /device:TPU:0, one launch (start us, length us, event | category | flops | bytes accessed | tf_op | source)
XLA Modules:
  0.0 346.3 jit_solution(9113034912710421854)
XLA Ops:
  6.5 1.3 fusion.31
  7.8 0.3 slice_reduce_fusion
  8.2 3.9 %copy.78 = bf16[512,2048]{0,1:T(8,128)(2,1)} copy(bf16[512,2048]{1,0:T(8,128)(2,1)} %param.14) | data formatting | bytes 4194304 | tf_op jit(solution)/shard_map/reshape | solution.py:406
  12.1 3.8 %fusion.21 = bf16[16,128,128]{2,1,0:T(8,128)(2,1)} fusion(bf16[512,16,128]{0,2,1:T(8,128)(2,1)} %bitcast.91, f32[512,16]{0,1:T(8,128)S(1)} %get-tuple-element.129, bf16[512,2048]{1,0:T(8,128)(2,1)} %param.15), kind=kOutput, calls=%fused_computation.32 | convolution fusion | flops 271843328 | bytes 4751360 | tf_op jit(solution)/shard_map/thd,the->hde/dot_general | solution.py:423
  16.0 0.2 fusion.35
  16.2 10.2 %all-gather.1 = bf16[8,1,16]{2,1,0:T(2,128)(2,1)S(1)} all-gather(bf16[1,1,16]{2,1,0:T(2,128)(2,1)S(1)} %bitcast.96), channel_id=1, replica_groups=mesh['ctx'=8,'exp'=4] {'ctx'}, dimensions={0}, use_global_device_ids=true | all-gather | bytes 288 | tf_op jit(solution)/shard_map/all_gather | solution.py:14
  26.5 10.3 %fusion.3 = f32[16,512,128]{1,2,0:T(8,128)} fusion(bf16[512,16,128]{0,2,1:T(8,128)(2,1)} %bitcast.92, f32[16,512]{1,0:T(8,128)S(1)} %bitcast.94, pred[512,512]{1,0:T(8,128)(4,1)S(1)} %iota_compare_fusion, bf16[512,2048]{1,0:T(8,128)(2,1)} %param.15, bf16[512,2048]{1,0:T(8,128)(2,1)S(1)} %copy-done), kind=kOutput, calls=%fused_computation.12 | convolution fusion | flops 2168455168 | bytes 10780672 | tf_op jit(solution)/shard_map/hts,shd->thd/dot_general | solution.py:418
  36.8 18.7 %all-gather.4.cloned.1.call-done = bf16[128,128,128]{2,1,0:T(8,128)(2,1)} async-done(((bf16[16,128,128]{2,1,0:T(8,128)(2,1)}), bf16[128,128,128]{2,1,0:T(8,128)(2,1)}) %all-gather.4.cloned.1.call-update) | async-done | bytes 4194320 | tf_op jit(solution)/shard_map/all_gather | solution.py:14
  55.5 10.6 %while.14 = (s32[]{:T(128)}, f32[16,128,128]{2,1,0:T(8,128)S(1)}, s32[]{:T(128)}, bf16[8,16]{1,0:T(8,128)(2,1)S(1)}, bf16[8,16,128,128]{3,2,1,0:T(8,128)(2,1)}, /*index=5*/s32[]{:T(128)}, s32[]{:T(128)}) while((s32[]{:T(128)}, f32[16,128,128]{2,1,0:T(8,128)S(1)}, s32[]{:T(128)}, bf16[8,16]{1,0:T(8,128)(2,1)S(1)}, ...), condition=%wide.region_1.2_spmd.clone, body=%wide.region_0.1_spmd.clone.sunk | while | flops 1310740 | bytes 2621705 | solution.py:31
  55.6 1.3 fusion.51
  56.9 1.3 fusion.51
  58.2 1.3 fusion.51
  59.5 1.3 fusion.51
  60.9 1.3 fusion.51
  62.2 1.3 fusion.51
  63.5 1.3 fusion.51
  64.9 1.3 fusion.51
  66.2 4.5 %multiply_reduce_fusion = (f32[512,16]{0,1:T(8,128)S(1)}, f32[512,16,128]{0,2,1:T(8,128)S(1)}) fusion(f32[16,128,128]{2,1,0:T(8,128)S(1)} %get-tuple-element.99, f32[512,16]{0,1:T(8,128)S(1)} %get-tuple-element.128, f32[16,512,128]{1,2,0:T(8,128)} %fusion.3, bf16[512,2048]{1,0:T(8,128)(2,1)S(1)} %copy-done), kind=kOutput, calls=%fused_computation.8 | convolution fusion | flops 1614798848 | bytes 11599872 | tf_op jit(solution)/shard_map/thd,hde->the/dot_general | solution.py:427
  70.7 0.6 multiply_convert_fusion
  71.4 11.0 %convolution_convert_fusion = bf16[512,3072]{1,0:T(8,128)(2,1)} fusion(bf16[512,2048]{0,1:T(8,128)(2,1)S(1)} %bitcast.90, bf16[2048,3072]{1,0:T(8,128)(2,1)} %param.18), kind=kOutput, calls=%fused_computation.4 | convolution fusion | flops 6444023808 | bytes 17825792 | tf_op jit(solution)/shard_map/dot_general | solution.py:438
  82.4 0.6 copy-done.5
  83.0 0.1 copy.72
  83.1 0.1 eq.59
  83.3 0.3 fusion.25
  83.6 0.1 reduce_sum.31
  83.9 58.9 %reduce-scatter.2.cloned.1.call-done = bf16[128,3072]{1,0:T(8,128)(2,1)} async-done(((bf16[512,3072]{1,0:T(8,128)(2,1)}), bf16[128,3072]{1,0:T(8,128)(2,1)}) %reduce-scatter.2.cloned.1.call-update) | async-done | bytes 786448 | tf_op jit(solution)/shard_map/reduce_scatter | solution.py:437
  142.8 1.5 multiply_reduce_fusion.1
  144.3 2.0 convolution_convert_fusion.1
  146.4 188.8 %shard_map.109 = bf16[4,80,3072]{2,1,0:T(8,128)(2,1)} custom-call(bf16[4,80,3072]{2,1,0:T(8,128)(2,1)} %bitcast.89, bf16[4,3072,768]{2,1,0:T(8,128)(2,1)} %w_gate.1, bf16[4,3072,768]{2,1,0:T(8,128)(2,1)} %w_up.1, bf16[4,768,3072]{2,1,0:T(8,128)(2,1)} %w_down.1), custom_call_target="tpu_custom_call" | custom-call | tf_op jit(solution)/shard_map/pallas_call | solution.py:359
  335.2 2.6 fusion.28
  337.9 1.4 fusion.19
  339.3 0.2 copy-done.1
  (35 shorter events, 0.5 us)
Async XLA Ops:
  6.5 20.0 %copy-start = (bf16[512,2048]{1,0:T(8,128)(2,1)S(1)}, bf16[512,2048]{1,0:T(8,128)(2,1)}, u32[]{:S(2)}) copy-start(bf16[512,2048]{1,0:T(8,128)(2,1)} %param.13) | copy-start | bytes 6291460
  6.5 49.0 %all-gather.4.cloned.1.call-start = ((), (), s32[]{:S(2)}) async-start(), calls=%async_computation.2 | async-start | bytes 4718592 | tf_op jit(solution)/shard_map/all_gather | solution.py:14
  16.0 126.8 %reduce-scatter.2.cloned.1.call-start = ((), (), s32[]{:S(2)}) async-start(), calls=%async_computation.1 | async-start | bytes 3932160 | tf_op jit(solution)/shard_map/reduce_scatter | solution.py:437
  82.3 0.7 copy-start.5
  82.3 1.5 copy-start.6
  82.3 60.4 %copy-start.2 = (bf16[128,3072]{1,0:T(8,128)(2,1)S(1)}, bf16[128,3072]{1,0:T(8,128)(2,1)}, u32[]{:S(2)}) copy-start(bf16[128,3072]{1,0:T(8,128)(2,1)} %param.17) | copy-start | bytes 2359300
  142.8 1.6 copy-start.3
  335.2 2.7 copy-start.4
  337.8 1.7 copy-start.1
Sparse Core Ops, SparseCore 0:
  16.1 39.4 all-gather.3
  82.5 60.2 reduce-scatter.1
